TPU v7x, 32 devices: a whole 2x2x4 slice. The times are simulated.
32 devices in a mesh: input: 8 (over z, core), crate: 4 (over y, x).
Axes of the slice: x: 2, y: 2, z: 4, core: 2. Of those that a mesh axis runs over, the one named last changes fastest.
Arguments:
- volts: bfloat16 [4, 16, 530432], P('crate', 'input'), may hold values from -6 to 6
- gains: bfloat16 [4, 16, 256], P('crate', 'input'), may hold values from -5 to 5
Outputs:
- visibility: float32 [128, 2, 64, 64], P('input', None, 'crate')
All inputs are finite; a program needn't handle non-finite values.
Results may differ from a plain program's by a relative error of at most 0.0026.
Values may be sent and summed in bfloat16 or wider, within the bound.
A program may use at most 64 MiB of HBM per device.

v0:
```python
import math

import jax
import jax.numpy as jnp
from jax import lax
from jax.sharding import PartitionSpec as P

FRAME = 2048
TAPS = 4
SUB = 128
SUB_START = 256
SPEC = 256


def window_table():
    length = TAPS * FRAME
    index = jnp.arange(length, dtype=jnp.float32)
    centred = (index - length / 2.0 + 0.5) / FRAME
    taper = 0.5 - 0.5 * jnp.cos(2.0 * math.pi * (index + 0.5) / length)
    return (jnp.sinc(centred) * taper).reshape(TAPS, FRAME)


def make_table():
    sample_idx = jnp.arange(FRAME, dtype=jnp.int32)
    chan_idx = SUB_START + jnp.arange(SUB, dtype=jnp.int32)
    product = sample_idx[:, None] * chan_idx[None, :] % FRAME
    phase = product.astype(jnp.float32) * (2.0 * math.pi / FRAME)
    norm_factor = 1.0 / math.sqrt(FRAME)
    return (jnp.concatenate([jnp.cos(phase), -jnp.sin(phase)], axis=1) * norm_factor).astype(
        jnp.bfloat16
    )


def channelize(volt_rows, gain_rows, window, dft_table):
    count = volt_rows.shape[0]
    frames = volt_rows.reshape(count, SPEC + TAPS - 1, FRAME).astype(jnp.float32)
    summed = jnp.zeros((count, SPEC, FRAME), jnp.float32)
    for tap_index in range(TAPS):
        summed = (
            summed + window[tap_index][None, None, :] * frames[:, tap_index : tap_index + SPEC, :]
        )
    weighted = summed.astype(jnp.bfloat16)
    raw_spec = jnp.dot(
        weighted.reshape(count * SPEC, FRAME), dft_table, preferred_element_type=jnp.float32
    )
    raw_spec = raw_spec.reshape(count, SPEC, 2 * SUB)
    gain_f = gain_rows.astype(jnp.float32)[:, None, :]
    real_part, imag_part = (raw_spec[..., :SUB], raw_spec[..., SUB:])
    gain_re, gain_im = (gain_f[..., :SUB], gain_f[..., SUB:])
    out_re = real_part * gain_re - imag_part * gain_im
    out_im = real_part * gain_im + imag_part * gain_re
    return jnp.stack([out_re, out_im], axis=2).astype(jnp.bfloat16)


def correlate_block(row_operand, piece):
    return jnp.einsum("fqrk,fck->fqrc", row_operand, piece, preferred_element_type=jnp.float32)


def shards(volts, gains):
    window = window_table()
    dft_table = make_table()
    spectra = channelize(volts[0], gains[0], window, dft_table)
    outgoing = spectra.transpose(3, 0, 2, 1)
    groups = lax.axis_size("input")
    channels = outgoing.shape[0] // groups
    local = lax.all_to_all(outgoing, "input", split_axis=0, concat_axis=1, tiled=True)
    rows = local.shape[1]
    columns = local.reshape(channels, rows, 2 * SPEC)
    flipped = jnp.concatenate([local[:, :, 1], -local[:, :, 0]], axis=-1)
    row_operand = jnp.stack([columns, flipped], axis=1)
    visibility = correlate_block(row_operand, lax.all_gather(columns, "crate", axis=1, tiled=True))
    return visibility * (1.0 / SPEC)


def solution(mesh):
    return jax.shard_map(
        shards,
        mesh=mesh,
        in_specs=(P("crate", "input", None), P("crate", "input", None)),
        out_specs=P("input", None, "crate", None),
        check_vma=False,
    )
```

profile of v0, /device:TPU:0, one launch (start us, length us, event | category | flops | bytes accessed | tf_op | source)
XLA Modules:
  0.0 76.4 jit_solution(1740348892998393471)
XLA Ops:
  6.5 0.0 all-gather.2.cloned.1.call-start
  6.5 0.2 fusion.28
  6.7 0.0 copy-start
  6.7 4.1 %fusion.20 = (f32[2048,128]{1,0:T(8,128)S(1)}, f32[2048,128]{1,0:T(8,128)S(1)}) fusion(s32[128]{0:T(128)S(1)} %iota_add_fusion.2), kind=kLoop, calls=%fused_computation.28 | loop fusion | flops 3932160 | bytes 2097664 | tf_op jit(solution)/shard_map/cos | solution.py:29
  10.9 4.7 %reshape.42 = f32[2,259,2048]{2,1,0:T(8,128)} reshape(bf16[1,2,530432]{2,1,0:T(2,128)(2,1)} %param.2) | data formatting | bytes 6365184 | tf_op jit(solution)/shard_map/convert_element_type | solution.py:36
  15.6 0.0 copy-done
  15.6 8.6 %fusion.5 = f32[2,256,256]{2,1,0:T(8,128)S(1)} fusion(f32[2,259,2048]{2,1,0:T(8,128)} %reshape.42, f32[2048]{0:T(1024)S(1)} %get-tuple-element.10, f32[2048]{0:T(1024)S(1)} %get-tuple-element.11, f32[2048]{0:T(1024)S(1)} %get-tuple-element.12, f32[2048]{0:T(1024)S(1)} %get-tuple-element.9, f32[2048,128]{1,0:T(8,128)S(1)} %get-tuple-element.16, ...), kind=kOutput, calls=%fused_computation.10 | convolution fusion | flops 546832384 | bytes 19431424 | tf_op jit(solution)/shard_map/dot_general | solution.py:43
  24.2 0.1 fusion.21
  24.3 0.2 copy.10
  24.5 15.9 %all_to_all.18 = bf16[128,2,2,256]{3,1,2,0:T(2,128)(2,1)S(1)} all-to-all(bf16[128,2,2,256]{3,1,2,0:T(2,128)(2,1)S(1)} %copy.10), channel_id=1, replica_groups=mesh['input'=8,'crate'=4] {'input'}, dimensions={0} | all-to-all | bytes 524288 | tf_op jit(solution)/shard_map/all_to_all | solution.py:66
  40.4 0.3 copy.12
  40.6 0.9 %reshape.41 = bf16[16,16,512]{2,1,0:T(8,128)(2,1)} reshape(bf16[16,8,2,2,256]{4,3,2,1,0:T(2,128)(2,1)S(1)} %copy.12) | data formatting | bytes 524288 | tf_op jit(solution)/shard_map/reshape | solution.py:68
  41.5 0.0 all-gather.2.cloned.1.call-update
  41.5 0.3 copy.13
  41.8 0.2 stack_reshape.3
  42.0 0.1 all_to_all.16
  42.2 25.1 %all-gather.2.cloned.1.call-done = bf16[16,64,512]{2,1,0:T(8,128)(2,1)} async-done(((bf16[16,16,512]{2,1,0:T(8,128)(2,1)}), bf16[16,64,512]{2,1,0:T(8,128)(2,1)}) %all-gather.2.cloned.1.call-update) | async-done | bytes 1048592 | tf_op jit(solution)/shard_map/all_gather | solution.py:71
  67.2 2.3 %convolution_multiply_fusion = f32[16,2,16,64]{3,2,1,0:T(8,128)} fusion(bf16[16,64,512]{2,1,0:T(8,128)(2,1)} %all-gather.2.cloned.1.call-done, bf16[16,1,16,512]{3,2,1,0:T(8,128)(2,1)S(1)} %maximum_bitcast_fusion.1, bf16[16,1,16,512]{3,2,1,0:T(8,128)(2,1)S(1)} %stack_reshape.3), kind=kOutput, calls=%fused_computation.14 | convolution fusion | flops 33849344 | bytes 1703936 | tf_op jit(solution)/shard_map/fqrk,fck->fqrc/dot_general | solution.py:56
  (8 shorter events, 0.1 us)
Async XLA Ops:
  6.5 60.7 %all-gather.2.cloned.1.call-start = ((), (), s32[]{:S(2)}) async-start(), calls=%async_computation.1 | async-start | bytes 1310720 | tf_op jit(solution)/shard_map/all_gather | solution.py:71
  6.7 8.8 %copy-start = (bf16[1,2,256]{2,1,0:T(2,128)(2,1)S(1)}, bf16[1,2,256]{2,1,0:T(2,128)(2,1)}, u32[]{:S(2)}) copy-start(bf16[1,2,256]{2,1,0:T(2,128)(2,1)} %param.3) | copy-start | bytes 3076
Sparse Core Ops, SparseCore 0:
  41.7 25.5 all-gather.1
where the time goes:
time: 76.6 us; the launch traced here: 76.4 us
  waiting for transfers between devices  25.1 us (33%)
  blocking collectives  15.9 us (21%)
  between operations  13.5 us (18%)
  matrix products  10.9 us (14%)
  local copies, waits for them, and re-layouts  6.62 us (9%)
  other arithmetic  4.45 us (6%)
    all_gather x1, waiting for transfers between devices, shards(): lax.all_gather(columns, 'crate', axis=1, tiled=True)  25.1 us
    all_to_all x1, blocking collectives, shards(): lax.all_to_all(outgoing, 'input', split_axis=0, concat_axis=1, tiled=True)  15.9 us
    dot_general x1, matrix products, channelize(): jnp.dot(weighted.reshape(count * SPEC, FRAME), dft_table, preferred_eleme...  8.56 us
    convert_element_type x1, local copies, waits for them, and re-layouts, channelize(): volt_rows.reshape(count, SPEC + TAPS - 1, FRAME).astype(jnp.float32)  4.69 us
    cos x1, other arithmetic, make_table(): jnp.cos(phase)  4.13 us
    dot_general x1, matrix products, correlate_block(): jnp.einsum('fqrk,fck->fqrc', row_operand, piece, preferred_element_type=j...  2.33 us
  transfers between devices with their start and end apart: 1, of which 1 were waited for; matrix products, arithmetic and copies ran while one was open for 1% of the time, Pallas kernels for 0%

commit v1 on v0

v1 whole, which is shorter than its diff:
```python
import functools
import math

import jax
import jax.numpy as jnp
import ml_dtypes
import numpy as np
from jax import lax
from jax.experimental import pallas as pl
from jax.experimental.pallas import tpu as pltpu
from jax.sharding import PartitionSpec as P

FRAME = 2048
TAPS = 4
SUB = 128
SUB_START = 256
SPEC = 256
LANES = 128
COLS = FRAME // LANES
FROWS = 2 * COLS
QUAD = 4
MESH = pl.DeviceIdType.MESH
NT = (((1,), (1,)), ((), ()))


def window_np():
    length = TAPS * FRAME
    index = np.arange(length, dtype=np.float64)
    centred = (index - length / 2.0 + 0.5) / FRAME
    taper = 0.5 - 0.5 * np.cos(2.0 * math.pi * (index + 0.5) / length)
    return (np.sinc(centred) * taper).reshape(TAPS, FRAME).astype(np.float32)


def table_np():
    sample_idx = np.arange(FRAME)
    chan_idx = SUB_START + np.arange(SUB)
    phase = (sample_idx[:, None] * chan_idx[None, :] % FRAME) * (2.0 * math.pi / FRAME)
    table = np.concatenate([np.cos(phase), -np.sin(phase)], axis=1) / math.sqrt(FRAME)
    return table.astype(np.float32).astype(ml_dtypes.bfloat16)


def channelize(volt_rows, gain_rows, window, dft_table):
    count = volt_rows.shape[0]
    frames = volt_rows.reshape(count, SPEC + TAPS - 1, FRAME).astype(jnp.float32)
    summed = jnp.zeros((count, SPEC, FRAME), jnp.float32)
    for tap_index in range(TAPS):
        summed = (
            summed + window[tap_index][None, None, :] * frames[:, tap_index : tap_index + SPEC, :]
        )
    weighted = summed.astype(jnp.bfloat16)
    raw_spec = jnp.dot(
        weighted.reshape(count * SPEC, FRAME), dft_table, preferred_element_type=jnp.float32
    )
    raw_spec = raw_spec.reshape(count, SPEC, 2 * SUB)
    gain_f = gain_rows.astype(jnp.float32)[:, None, :]
    real_part, imag_part = (raw_spec[..., :SUB], raw_spec[..., SUB:])
    gain_re, gain_im = (gain_f[..., :SUB], gain_f[..., SUB:])
    out_re = real_part * gain_re - imag_part * gain_im
    out_im = real_part * gain_im + imag_part * gain_re
    return jnp.stack([out_re, out_im], axis=2).astype(jnp.bfloat16)


def general_shards(volts, gains):
    spectra = channelize(volts[0], gains[0], jnp.asarray(window_np()), jnp.asarray(table_np()))
    outgoing = spectra.transpose(3, 0, 2, 1)
    groups = lax.axis_size("input")
    channels = outgoing.shape[0] // groups
    local = lax.all_to_all(outgoing, "input", split_axis=0, concat_axis=1, tiled=True)
    rows = local.shape[1]
    columns = local.reshape(channels, rows, 2 * SPEC)
    flipped = jnp.concatenate([local[:, :, 1], -local[:, :, 0]], axis=-1)
    row_operand = jnp.stack([columns, flipped], axis=1)
    gathered = lax.all_gather(columns, "crate", axis=1, tiled=True)
    visibility = jnp.einsum(
        "fqrk,fck->fqrc", row_operand, gathered, preferred_element_type=jnp.float32
    )
    return visibility * (1.0 / SPEC)


def kernel(
    groups, crates, volts_hbm, gains_ref, window_ref, table_hbm, pick_hbm, out_ref,
    raw, table, pick, fir, outgoing, arrived, wide, vis_out, load_sem, table_sem, pick_sem,
    send_sem, recv_sem, vsend_sem, vrecv_sem,
):
    n = groups * crates
    g, r = lax.axis_index("input"), lax.axis_index("crate")
    own = g * crates + r
    source = r * groups + g

    pieces = load_sem.shape[0]
    step = SPEC // pieces

    def load(k):
        start = 0 if k == 0 else (k * step + TAPS - 1) * FROWS
        stop = ((k + 1) * step + TAPS - 1) * FROWS
        rows = pl.ds(start, stop - start)
        return pltpu.make_async_copy(volts_hbm.at[rows], raw.at[rows], load_sem.at[k])

    loads = [load(k) for k in range(pieces)]
    loads[0].start()
    table_load = pltpu.make_async_copy(table_hbm, table, table_sem)
    pick_load = pltpu.make_async_copy(pick_hbm, pick, pick_sem)
    for item in loads[1:]:
        item.start()
    table_load.start()
    pick_load.start()

    barrier = pltpu.get_barrier_semaphore()

    @pl.loop(1, n)
    def _(k):
        other = lax.rem(own + k, n)
        pl.semaphore_signal(
            barrier, inc=1, device_id=(other // crates, lax.rem(other, crates)), device_id_type=MESH
        )

    taps = [window_ref[p] for p in range(TAPS)]

    def frame(t):
        return raw[pl.ds(pl.multiple_of(t * FROWS, FROWS), FROWS), :].astype(jnp.float32)

    for k in range(pieces):
        loads[k].wait()

        def body(s, held, k=k):
            held = list(held)
            for u in range(8):
                t = k * step + s * 8 + u
                held.append(frame(t + TAPS - 1))
                total = taps[0] * held[0]
                for p in range(1, TAPS):
                    total = total + taps[p] * held[p]
                fir[pl.ds(pl.multiple_of(t * FROWS, FROWS), FROWS), :] = total
                held = held[1:]
            return tuple(held)

        lax.fori_loop(0, step // 8, body, tuple(frame(k * step + p) for p in range(TAPS - 1)))

    table_load.wait()
    pick_load.wait()
    halves = []
    for i in range(2):
        total = jnp.zeros((2 * SUB, SPEC), jnp.float32)
        for c in range(0, COLS, 2):
            weighted = jnp.concatenate(
                [fir[pl.ds(2 * (c + e) + i, SPEC, stride=FROWS), :] for e in range(2)], axis=1
            ).astype(jnp.bfloat16)
            total = total + lax.dot_general(
                table[:, c * LANES : (c + 2) * LANES], weighted, NT,
                preferred_element_type=jnp.float32,
            )
        spread = jnp.broadcast_to(
            gains_ref[i : i + 1, :].astype(jnp.float32), (LANES, 2 * SUB)
        ).astype(jnp.bfloat16)
        gain = lax.dot_general(pick[...], spread, NT, preferred_element_type=jnp.float32)
        straight = jnp.concatenate([gain[: 2 * SUB]] * (SPEC // LANES), axis=1)
        crossed = jnp.concatenate([gain[2 * SUB :]] * (SPEC // LANES), axis=1)
        total = total.reshape(n, 2 * QUAD, SPEC)
        swapped = jnp.concatenate([total[:, QUAD:], total[:, :QUAD]], axis=1)
        halves.append(
            total * straight.reshape(n, 2 * QUAD, SPEC) + swapped * crossed.reshape(n, 2 * QUAD, SPEC)
        )
    outgoing[...] = jnp.concatenate(halves, axis=1).astype(jnp.bfloat16)

    pl.semaphore_wait(barrier, n - 1)

    @pl.loop(1, n)
    def _(k):
        other = lax.rem(own + k, n)
        pltpu.make_async_remote_copy(
            src_ref=outgoing.at[other],
            dst_ref=arrived.at[source],
            send_sem=send_sem,
            recv_sem=recv_sem,
            device_id=(other // crates, lax.rem(other, crates)),
            device_id_type=MESH,
        ).start()

    arrived[source] = outgoing[own]
    rest = pl.ds(0, n - 1)
    pltpu.make_async_copy(outgoing.at[rest], arrived.at[rest], recv_sem).wait()

    blocks = SPEC // LANES
    for e in range(blocks):
        part = arrived[:, :, e * LANES : (e + 1) * LANES].astype(jnp.float32)
        wide[e] = part.reshape(wide.shape[1:])
    inputs = 2 * n
    rows = inputs // crates
    for q in range(QUAD):
        real = [wide[e, pl.ds(q, inputs, stride=2 * QUAD), :] for e in range(blocks)]
        imag = [wide[e, pl.ds(QUAD + q, inputs, stride=2 * QUAD), :] for e in range(blocks)]
        left = jnp.concatenate(real + imag, axis=1).astype(jnp.bfloat16)
        turned = jnp.concatenate([-x for x in imag] + real, axis=1).astype(jnp.bfloat16)
        right = jnp.concatenate([left, turned], axis=0)
        vis = lax.dot_general(left, right, NT, preferred_element_type=jnp.float32) * (1.0 / SPEC)
        vis_out[:, q] = vis.reshape(crates, rows, 2 * inputs)

    for k in range(1, crates):
        other = lax.rem(r + k, crates)
        pltpu.make_async_remote_copy(
            src_ref=vis_out.at[other],
            dst_ref=out_ref.at[r],
            send_sem=vsend_sem,
            recv_sem=vrecv_sem,
            device_id=(g, other),
            device_id_type=MESH,
        ).start()
    out_ref[r] = vis_out[r]
    rest_v = pl.ds(0, crates - 1)
    pltpu.make_async_copy(vis_out.at[rest_v], out_ref.at[rest_v], vrecv_sem).wait()
    pltpu.make_async_copy(vis_out.at[rest_v], out_ref.at[rest_v], vsend_sem).wait()
    pltpu.make_async_copy(outgoing.at[rest], arrived.at[rest], send_sem).wait()


def quad_shards(groups, crates, volts, gains):
    n = groups * crates
    inputs = 2 * n
    rows = inputs // crates
    order = np.arange(2 * SUB).reshape(2, n, QUAD).transpose(1, 0, 2).reshape(-1)
    table = np.ascontiguousarray(table_np().T[order])
    chan = order % SUB
    imag = order >= SUB
    pick = np.zeros((2, 2 * SUB, 2 * SUB), np.float32)
    at = np.arange(2 * SUB)
    pick[0, at, chan] = 1.0
    pick[1, at, SUB + chan] = np.where(imag, 1.0, -1.0)
    pick = pick.reshape(4 * SUB, 2 * SUB).astype(ml_dtypes.bfloat16)
    window = np.repeat(window_np().reshape(TAPS, COLS, LANES), 2, axis=1)
    frames = volts.shape[-1] // LANES
    stacked = volts.reshape(2, frames, LANES).transpose(1, 0, 2).reshape(2 * frames, LANES)
    hbm = pl.BlockSpec(memory_space=pltpu.HBM)
    vmem = pl.BlockSpec(memory_space=pltpu.VMEM)
    pieces = 4
    vis = pl.pallas_call(
        functools.partial(kernel, groups, crates),
        out_shape=jax.ShapeDtypeStruct((crates, QUAD, rows, 2 * inputs), jnp.float32),
        in_specs=[hbm, vmem, vmem, hbm, hbm],
        out_specs=vmem,
        scratch_shapes=[
            pltpu.VMEM((2 * frames, LANES), jnp.bfloat16),
            pltpu.VMEM((2 * SUB, FRAME), jnp.bfloat16),
            pltpu.VMEM((4 * SUB, 2 * SUB), jnp.bfloat16),
            pltpu.VMEM((SPEC * FROWS, LANES), jnp.float32),
            pltpu.VMEM((n, 4 * QUAD, SPEC), jnp.bfloat16),
            pltpu.VMEM((n, 4 * QUAD, SPEC), jnp.bfloat16),
            pltpu.VMEM((SPEC // LANES, n * 4 * QUAD, LANES), jnp.float32),
            pltpu.VMEM((crates, QUAD, rows, 2 * inputs), jnp.float32),
            pltpu.SemaphoreType.DMA((pieces,)),
            pltpu.SemaphoreType.DMA,
            pltpu.SemaphoreType.DMA,
            pltpu.SemaphoreType.DMA,
            pltpu.SemaphoreType.DMA,
            pltpu.SemaphoreType.DMA,
            pltpu.SemaphoreType.DMA,
        ],
        compiler_params=pltpu.CompilerParams(
            collective_id=0, has_side_effects=True, vmem_limit_bytes=40 * 1024 * 1024
        ),
    )(stacked, gains[0], jnp.asarray(window), jnp.asarray(table), jnp.asarray(pick))
    vis = vis.reshape(crates * QUAD, rows, 2, inputs)
    return vis.transpose(0, 2, 1, 3)


def solution(mesh):
    groups, crates = mesh.shape["input"], mesh.shape["crate"]
    shards = general_shards
    if groups * crates * QUAD == SUB:
        shards = functools.partial(quad_shards, groups, crates)
    return jax.shard_map(
        shards,
        mesh=mesh,
        in_specs=(P("crate", "input", None), P("crate", "input", None)),
        out_specs=P("input", None, "crate", None),
        check_vma=False,
    )
```

time: 76.6 us -> 25.7 us (0.34)
  waiting for transfers between devices: 25.1 us -> 0 us
  Pallas kernels: 0 us -> 19.2 us
  blocking collectives: 15.9 us -> 0 us
  between operations: 13.5 us -> 0.02 us
  matrix products: 10.9 us -> 0 us
  other arithmetic: 4.45 us -> 0 us
    all_gather x1 -> x0, waiting for transfers between devices: 25.1 us -> none  [shards(): lax.all_gather(columns, 'crate', axis=1, tiled=True)]
    pallas_call x0 -> x1, Pallas kernels: none -> 19.2 us  [quad_shards(): pl.pallas_call(functools.partial(kernel, groups, crates), out_shape=jax.S...]
    all_to_all x1 -> x0, blocking collectives: 15.9 us -> none  [shards(): lax.all_to_all(outgoing, 'input', split_axis=0, concat_axis=1, tiled=True)]
    dot_general x2 -> x0, matrix products: 10.9 us -> none  [the longest x1 8.56 us: channelize(): jnp.dot(weighted.reshape(count * SPEC, FRAME), dft_table, preferred_eleme...]
    unnamed x2 -> x10, local copies, waits for them, and re-layouts: 0.01 us -> 5.29 us
    convert_element_type x1 -> x0, local copies, waits for them, and re-layouts: 4.69 us -> none  [channelize(): volt_rows.reshape(count, SPEC + TAPS - 1, FRAME).astype(jnp.float32)]
    cos x1 -> x0, other arithmetic: 4.13 us -> none  [make_table(): jnp.cos(phase)]
  transfers between devices with their start and end apart: 1 -> 0, of which waited for: 1 -> 0; matrix products, arithmetic and copies ran while one was open for 1% -> 0% of each run, Pallas kernels for 0% -> 0%
where the time goes in v1:
time: 25.7 us; the launch traced here: 25.4 us
  Pallas kernels  19.2 us (75%)
  local copies, waits for them, and re-layouts  6.2 us (24%)
    pallas_call x1, Pallas kernels, quad_shards(): pl.pallas_call(functools.partial(kernel, groups, crates), out_shape=jax.S...  19.2 us
    unnamed x10, local copies, waits for them, and re-layouts  5.29 us
    reshape x2, local copies, waits for them, and re-layouts, quad_shards(): vis = vis.reshape(crates * QUAD, rows, 2, inputs)  0.91 us

profile of v1, /device:TPU:0, one launch (start us, length us, event | category | flops | bytes accessed | tf_op | source)
XLA Modules:
  0.0 25.4 jit_solution(10710615799861020242)
XLA Ops:
  0.0 0.0 copy-start
  0.0 1.6 %copy-done = bf16[1,2,530432]{2,1,0:T(2,128)(2,1)S(1)} copy-done((bf16[1,2,530432]{2,1,0:T(2,128)(2,1)S(1)}, bf16[1,2,530432]{2,1,0:T(2,128)(2,1)}, u32[]{:S(2)}) %copy-start) | copy-done | bytes 2121752
  1.6 0.0 copy-start.1
  1.6 1.2 %copy-done.1 = bf16[256,2048]{1,0:T(8,128)(2,1)S(1)} copy-done((bf16[256,2048]{1,0:T(8,128)(2,1)S(1)}, bf16[256,2048]{1,0:T(8,128)(2,1)}, u32[]{:S(2)}) %copy-start.1) | copy-done | bytes 1048600
  2.8 0.0 copy-start.2
  2.8 0.9 %copy-done.2 = bf16[512,256]{1,0:T(8,128)(2,1)S(1)} copy-done((bf16[512,256]{1,0:T(8,128)(2,1)S(1)}, bf16[512,256]{1,0:T(8,128)(2,1)}, u32[]{:S(2)}) %copy-start.2) | copy-done | bytes 262168
  3.8 0.0 copy-start.3
  3.8 0.8 %copy-done.3 = f32[4,32,128]{2,1,0:T(8,128)S(1)} copy-done((f32[4,32,128]{2,1,0:T(8,128)S(1)}, f32[4,32,128]{2,1,0:T(8,128)}, u32[]{:S(2)}) %copy-start.3) | copy-done | bytes 65560
  4.6 0.0 copy-start.4
  4.6 0.7 %copy-done.4 = bf16[1,2,256]{2,1,0:T(2,128)(2,1)S(1)} copy-done((bf16[1,2,256]{2,1,0:T(2,128)(2,1)S(1)}, bf16[1,2,256]{2,1,0:T(2,128)(2,1)}, u32[]{:S(2)}) %copy-start.4) | copy-done | bytes 1048
  5.3 19.2 %shard_map.55 = f32[4,4,16,128]{3,2,1,0:T(8,128)S(1)} custom-call(bf16[8288,128]{1,0:T(8,128)(2,1)S(1)} %bitcast.11, bf16[2,256]{1,0:T(2,128)(2,1)S(1)} %bitcast.12, f32[4,32,128]{2,1,0:T(8,128)S(1)} %copy-done.3, bf16[256,2048]{1,0:T(8,128)(2,1)S(1)} %copy-done.1, bf16[512,256]{1,0:T(8,128)(2,1)S(1)} %copy-done.2), custom_call_target="tpu_custom_call" | custom-call | tf_op jit(solution)/shard_map/pallas_call | solution.py:234
  24.5 0.2 reshape.11
  24.7 0.7 %copy.9 = f32[16,16,2,64]{3,1,2,0:T(8,128)} copy(f32[16,16,2,64]{3,2,1,0:T(2,128)S(1)} %reshape.11) | data formatting | bytes 262144 | tf_op jit(solution)/shard_map/reshape | solution.py:260
Async XLA Ops:
  0.0 1.6 %copy-start = (bf16[1,2,530432]{2,1,0:T(2,128)(2,1)S(1)}, bf16[1,2,530432]{2,1,0:T(2,128)(2,1)}, u32[]{:S(2)}) copy-start(bf16[1,2,530432]{2,1,0:T(2,128)(2,1)} %param.5) | copy-start | bytes 6365188
  1.6 1.2 %copy-start.1 = (bf16[256,2048]{1,0:T(8,128)(2,1)S(1)}, bf16[256,2048]{1,0:T(8,128)(2,1)}, u32[]{:S(2)}) copy-start(bf16[256,2048]{1,0:T(8,128)(2,1)} %constant.7.clone.table_hbm) | copy-start | bytes 3145732
  2.8 0.9 %copy-start.2 = (bf16[512,256]{1,0:T(8,128)(2,1)S(1)}, bf16[512,256]{1,0:T(8,128)(2,1)}, u32[]{:S(2)}) copy-start(bf16[512,256]{1,0:T(8,128)(2,1)} %constant.8.clone.pick_hbm) | copy-start | bytes 786436
  3.8 0.8 %copy-start.3 = (f32[4,32,128]{2,1,0:T(8,128)S(1)}, f32[4,32,128]{2,1,0:T(8,128)}, u32[]{:S(2)}) copy-start(f32[4,32,128]{2,1,0:T(8,128)} %constant.6.clone.window_ref) | copy-start | bytes 196612
  4.6 0.7 %copy-start.4 = (bf16[1,2,256]{2,1,0:T(2,128)(2,1)S(1)}, bf16[1,2,256]{2,1,0:T(2,128)(2,1)}, u32[]{:S(2)}) copy-start(bf16[1,2,256]{2,1,0:T(2,128)(2,1)} %param.6) | copy-start | bytes 3076

commit v2 on v1

v2 whole, which is shorter than its diff:
```python
import functools
import math

import jax
import jax.numpy as jnp
import ml_dtypes
import numpy as np
from jax import lax
from jax.experimental import pallas as pl
from jax.experimental.pallas import tpu as pltpu
from jax.sharding import PartitionSpec as P

FRAME = 2048
TAPS = 4
SUB = 128
SUB_START = 256
SPEC = 256
LANES = 128
COLS = FRAME // LANES
FROWS = 2 * COLS
QUAD = 4
CHUNKS = SPEC // LANES
STRIDE = FROWS + 1
MESH = pl.DeviceIdType.MESH
NT = (((1,), (1,)), ((), ()))


def window_np():
    length = TAPS * FRAME
    index = np.arange(length, dtype=np.float64)
    centred = (index - length / 2.0 + 0.5) / FRAME
    taper = 0.5 - 0.5 * np.cos(2.0 * math.pi * (index + 0.5) / length)
    return (np.sinc(centred) * taper).reshape(TAPS, FRAME).astype(np.float32)


def table_np():
    sample_idx = np.arange(FRAME)
    chan_idx = SUB_START + np.arange(SUB)
    phase = (sample_idx[:, None] * chan_idx[None, :] % FRAME) * (2.0 * math.pi / FRAME)
    table = np.concatenate([np.cos(phase), -np.sin(phase)], axis=1) / math.sqrt(FRAME)
    return table.astype(np.float32).astype(ml_dtypes.bfloat16)


def channelize(volt_rows, gain_rows, window, dft_table):
    count = volt_rows.shape[0]
    frames = volt_rows.reshape(count, SPEC + TAPS - 1, FRAME).astype(jnp.float32)
    summed = jnp.zeros((count, SPEC, FRAME), jnp.float32)
    for tap_index in range(TAPS):
        summed = (
            summed + window[tap_index][None, None, :] * frames[:, tap_index : tap_index + SPEC, :]
        )
    weighted = summed.astype(jnp.bfloat16)
    raw_spec = jnp.dot(
        weighted.reshape(count * SPEC, FRAME), dft_table, preferred_element_type=jnp.float32
    )
    raw_spec = raw_spec.reshape(count, SPEC, 2 * SUB)
    gain_f = gain_rows.astype(jnp.float32)[:, None, :]
    real_part, imag_part = (raw_spec[..., :SUB], raw_spec[..., SUB:])
    gain_re, gain_im = (gain_f[..., :SUB], gain_f[..., SUB:])
    out_re = real_part * gain_re - imag_part * gain_im
    out_im = real_part * gain_im + imag_part * gain_re
    return jnp.stack([out_re, out_im], axis=2).astype(jnp.bfloat16)


def general_shards(volts, gains):
    spectra = channelize(volts[0], gains[0], jnp.asarray(window_np()), jnp.asarray(table_np()))
    outgoing = spectra.transpose(3, 0, 2, 1)
    groups = lax.axis_size("input")
    channels = outgoing.shape[0] // groups
    local = lax.all_to_all(outgoing, "input", split_axis=0, concat_axis=1, tiled=True)
    rows = local.shape[1]
    columns = local.reshape(channels, rows, 2 * SPEC)
    flipped = jnp.concatenate([local[:, :, 1], -local[:, :, 0]], axis=-1)
    row_operand = jnp.stack([columns, flipped], axis=1)
    gathered = lax.all_gather(columns, "crate", axis=1, tiled=True)
    visibility = jnp.einsum(
        "fqrk,fck->fqrc", row_operand, gathered, preferred_element_type=jnp.float32
    )
    return visibility * (1.0 / SPEC)


def kernel(
    groups, crates, volts_hbm, gains_hbm, window_hbm, table_hbm, pick_hbm, out_ref,
    raw, gains_ref, window_ref, table, pick, fir, outgoing, arrived, wide, vis_out, vis_in, load_sem, side_sem,
    send_sem, recv_sem, vsend_sem, vrecv_sem,
):
    n = groups * crates
    g, r = lax.axis_index("input"), lax.axis_index("crate")
    own = g * crates + r
    source = r * groups + g

    pieces = load_sem.shape[0]
    step = SPEC // pieces

    def load(k):
        start = 0 if k == 0 else (k * step + TAPS - 1) * FROWS
        stop = ((k + 1) * step + TAPS - 1) * FROWS
        rows = pl.ds(start, stop - start)
        return pltpu.make_async_copy(volts_hbm.at[rows], raw.at[rows], load_sem.at[k])

    loads = [load(k) for k in range(pieces)]
    sides = [
        pltpu.make_async_copy(src, dst, side_sem.at[k])
        for k, (src, dst) in enumerate(
            [(window_hbm, window_ref), (gains_hbm, gains_ref), (pick_hbm, pick), (table_hbm, table)]
        )
    ]
    head = pieces // CHUNKS
    for item in [*sides[:3], *loads[:head], sides[3], *loads[head:]]:
        item.start()

    barrier = pltpu.get_barrier_semaphore()

    @pl.loop(1, n)
    def _(k):
        other = lax.rem(own + k, n)
        pl.semaphore_signal(
            barrier, inc=1, device_id=(other // crates, lax.rem(other, crates)), device_id_type=MESH
        )

    sides[1].wait()
    sides[2].wait()
    gain = []
    for i in range(2):
        spread = jnp.broadcast_to(
            gains_ref[i : i + 1, :].astype(jnp.float32), (LANES, 2 * SUB)
        ).astype(jnp.bfloat16)
        spread = lax.dot_general(pick[...], spread, NT, preferred_element_type=jnp.float32)
        gain.append(spread.reshape(2, n, 2 * QUAD, LANES))

    sides[0].wait()
    taps = [window_ref[p] for p in range(TAPS)]

    def frame(t):
        return raw[pl.ds(pl.multiple_of(t * FROWS, FROWS), FROWS), :].astype(jnp.float32)

    def filtered(k):
        def body(s, held):
            held = list(held)
            base = pl.multiple_of((k * step + s * 8) * STRIDE, 8)
            for u in range(8):
                held.append(frame(k * step + s * 8 + u + TAPS - 1))
                total = taps[0] * held[0]
                for p in range(1, TAPS):
                    total = total + taps[p] * held[p]
                fir[pl.ds(base + u * STRIDE, FROWS), :] = total
                held = held[1:]
            return tuple(held)

        lax.fori_loop(0, step // 8, body, tuple(frame(k * step + p) for p in range(TAPS - 1)))

    span = SPEC // CHUNKS
    rest = pl.ds(0, n - 1)
    for h in range(CHUNKS):
        for k in range(h * head, (h + 1) * head):
            loads[k].wait()
            filtered(k)
        if h == 0:
            sides[3].wait()
        total = jnp.zeros((2 * SUB, 2 * span), jnp.float32)
        for c in range(0, COLS, 2):
            weighted = jnp.concatenate(
                [
                    jnp.concatenate(
                        [
                            fir[pl.ds(h * span * STRIDE + 2 * (c + e) + i, span, stride=STRIDE), :]
                            for e in range(2)
                        ],
                        axis=1,
                    )
                    for i in range(2)
                ],
                axis=0,
            ).astype(jnp.bfloat16)
            total = total + lax.dot_general(
                table[:, c * LANES : (c + 2) * LANES], weighted, NT,
                preferred_element_type=jnp.float32,
            )
        halves = []
        for i in range(2):
            part = total[:, i * span : (i + 1) * span].reshape(n, 2 * QUAD, span)
            swapped = jnp.concatenate([part[:, QUAD:], part[:, :QUAD]], axis=1)
            halves.append(part * gain[i][0] + swapped * gain[i][1])
        outgoing[h] = jnp.concatenate(halves, axis=1).astype(jnp.bfloat16)

        if h == 0:
            pl.semaphore_wait(barrier, n - 1)

        @pl.loop(1, n)
        def _(k, h=h):
            other = lax.rem(own + k, n)
            pltpu.make_async_remote_copy(
                src_ref=outgoing.at[h, other],
                dst_ref=arrived.at[h, source],
                send_sem=send_sem.at[h],
                recv_sem=recv_sem.at[h],
                device_id=(other // crates, lax.rem(other, crates)),
                device_id_type=MESH,
            ).start()

        arrived[h, source] = outgoing[h, own]

    for h in range(CHUNKS):
        pltpu.make_async_copy(outgoing.at[h, rest], arrived.at[h, rest], recv_sem.at[h]).wait()
        wide[h, : n * 4 * QUAD] = arrived[h].astype(jnp.float32).reshape(n * 4 * QUAD, LANES)

    inputs = 2 * n
    rows = inputs // crates
    for q in range(QUAD):
        real = [wide[h, pl.ds(q, inputs, stride=2 * QUAD), :] for h in range(CHUNKS)]
        imag = [wide[h, pl.ds(QUAD + q, inputs, stride=2 * QUAD), :] for h in range(CHUNKS)]
        left = jnp.concatenate(real + imag, axis=1).astype(jnp.bfloat16)
        turned = jnp.concatenate([-x for x in imag] + real, axis=1).astype(jnp.bfloat16)
        right = jnp.concatenate([left, turned], axis=0)
        vis = lax.dot_general(left, right, NT, preferred_element_type=jnp.float32) * (1.0 / SPEC)
        vis_out[:, q] = vis.reshape(crates, rows, 2 * inputs)
        for k in range(1, crates):
            other = lax.rem(r + k, crates)
            pltpu.make_async_remote_copy(
                src_ref=vis_out.at[other, q],
                dst_ref=vis_in.at[r, q],
                send_sem=vsend_sem,
                recv_sem=vrecv_sem,
                device_id=(g, other),
                device_id_type=MESH,
            ).start()

    vis_in[r] = vis_out[r]
    rest_v = pl.ds(0, crates - 1)
    pltpu.make_async_copy(vis_out.at[rest_v], vis_in.at[rest_v], vrecv_sem).wait()
    whole = vis_in[...].reshape(crates * QUAD, rows, 2 * inputs)
    out_ref[:, 0] = whole[:, :, :inputs]
    out_ref[:, 1] = whole[:, :, inputs:]
    pltpu.make_async_copy(vis_out.at[rest_v], vis_in.at[rest_v], vsend_sem).wait()
    for h in range(CHUNKS):
        pltpu.make_async_copy(outgoing.at[h, rest], arrived.at[h, rest], send_sem.at[h]).wait()


def quad_shards(groups, crates, volts, gains):
    n = groups * crates
    inputs = 2 * n
    rows = inputs // crates
    order = np.arange(2 * SUB).reshape(2, n, QUAD).transpose(1, 0, 2).reshape(-1)
    table = np.ascontiguousarray(table_np().T[order])
    chan = order % SUB
    imag = order >= SUB
    pick = np.zeros((2, 2 * SUB, 2 * SUB), np.float32)
    at = np.arange(2 * SUB)
    pick[0, at, chan] = 1.0
    pick[1, at, SUB + chan] = np.where(imag, 1.0, -1.0)
    pick = pick.reshape(4 * SUB, 2 * SUB).astype(ml_dtypes.bfloat16)
    window = np.repeat(window_np().reshape(TAPS, COLS, LANES), 2, axis=1)
    frames = volts.shape[-1] // LANES
    stacked = volts.reshape(2, frames, LANES).transpose(1, 0, 2).reshape(2 * frames, LANES)
    hbm = pl.BlockSpec(memory_space=pltpu.HBM)
    vmem = pl.BlockSpec(memory_space=pltpu.VMEM)
    pieces = 4
    return pl.pallas_call(
        functools.partial(kernel, groups, crates),
        out_shape=jax.ShapeDtypeStruct((crates * QUAD, 2, rows, inputs), jnp.float32),
        in_specs=[hbm] * 5,
        out_specs=vmem,
        scratch_shapes=[
            pltpu.VMEM((2 * frames, LANES), jnp.bfloat16),
            pltpu.VMEM((2, 2 * SUB), jnp.bfloat16),
            pltpu.VMEM((TAPS, FROWS, LANES), jnp.float32),
            pltpu.VMEM((2 * SUB, FRAME), jnp.bfloat16),
            pltpu.VMEM((4 * SUB, 2 * SUB), jnp.bfloat16),
            pltpu.VMEM(((SPEC + 2) * STRIDE, LANES), jnp.float32),
            pltpu.VMEM((CHUNKS, n, 4 * QUAD, LANES), jnp.bfloat16),
            pltpu.VMEM((CHUNKS, n, 4 * QUAD, LANES), jnp.bfloat16),
            pltpu.VMEM((CHUNKS, (n + 1) * 4 * QUAD, LANES), jnp.float32),
            pltpu.VMEM((crates, QUAD, rows, 2 * inputs), jnp.float32),
            pltpu.VMEM((crates, QUAD, rows, 2 * inputs), jnp.float32),
            pltpu.SemaphoreType.DMA((pieces,)),
            pltpu.SemaphoreType.DMA((4,)),
            pltpu.SemaphoreType.DMA((CHUNKS,)),
            pltpu.SemaphoreType.DMA((CHUNKS,)),
            pltpu.SemaphoreType.DMA,
            pltpu.SemaphoreType.DMA,
        ],
        compiler_params=pltpu.CompilerParams(
            collective_id=0, has_side_effects=True, vmem_limit_bytes=60 * 1024 * 1024
        ),
    )(stacked, gains[0], jnp.asarray(window), jnp.asarray(table), jnp.asarray(pick))


def solution(mesh):
    groups, crates = mesh.shape["input"], mesh.shape["crate"]
    shards = general_shards
    if groups * crates * QUAD == SUB:
        shards = functools.partial(quad_shards, groups, crates)
    return jax.shard_map(
        shards,
        mesh=mesh,
        in_specs=(P("crate", "input", None), P("crate", "input", None)),
        out_specs=P("input", None, "crate", None),
        check_vma=False,
    )
```

time: 25.7 us -> 21.1 us (0.82)
  local copies, waits for them, and re-layouts: 6.2 us -> 1.67 us
    unnamed x10 -> x1, local copies, waits for them, and re-layouts: 5.29 us -> 1.67 us
    reshape x2 -> x0, local copies, waits for them, and re-layouts: 0.91 us -> none  [quad_shards(): vis = vis.reshape(crates * QUAD, rows, 2, inputs)]
where the time goes in v2:
time: 21.1 us; the launch traced here: 20.9 us
  Pallas kernels  19.3 us (91%)
  local copies, waits for them, and re-layouts  1.67 us (8%)
    pallas_call x1, Pallas kernels, quad_shards(): pl.pallas_call(functools.partial(kernel, groups, crates), out_shape=jax.S...  19.3 us
    unnamed x1, local copies, waits for them, and re-layouts  1.67 us

profile of v2, /device:TPU:0, one launch (start us, length us, event | category | flops | bytes accessed | tf_op | source)
XLA Modules:
  0.0 20.9 jit_solution(4598041390537907164)
XLA Ops:
  0.0 19.3 %shard_map.55 = f32[16,2,16,64]{3,2,1,0:T(8,128)} custom-call(bf16[8288,128]{1,0:T(8,128)(2,1)} %bitcast.6, bf16[2,256]{1,0:T(2,128)(2,1)} %bitcast.7, f32[4,32,128]{2,1,0:T(8,128)} %constant.6.clone.window_hbm, bf16[256,2048]{1,0:T(8,128)(2,1)} %constant.7.clone.table_hbm, bf16[512,256]{1,0:T(8,128)(2,1)} %constant.8.clone.pick_hbm), custom_call_target="tpu_custom_call" | custom-call | tf_op jit(solution)/shard_map/pallas_call | solution.py:258
  19.3 1.7 %copy.8 = f32[16,2,16,64]{3,2,1,0:T(8,128)} copy(f32[16,2,16,64]{3,2,1,0:T(8,128)} %shard_map.55) | data formatting | bytes 262144

commit v3 on v2

--- a/solution.py
+++ b/solution.py
@@ -257,7 +257,7 @@
     pieces = 4
     return pl.pallas_call(
         functools.partial(kernel, groups, crates),
-        out_shape=jax.ShapeDtypeStruct((crates * QUAD, 2, rows, inputs), jnp.float32),
+        out_shape=pltpu.VMEM((crates * QUAD, 2, rows, inputs), jnp.float32),
         in_specs=[hbm] * 5,
         out_specs=vmem,
         scratch_shapes=[
@@ -280,7 +280,7 @@
             pltpu.SemaphoreType.DMA,
         ],
         compiler_params=pltpu.CompilerParams(
-            collective_id=0, has_side_effects=True, vmem_limit_bytes=60 * 1024 * 1024
+            collective_id=0, has_side_effects=True, vmem_limit_bytes=57000000
         ),
     )(stacked, gains[0], jnp.asarray(window), jnp.asarray(table), jnp.asarray(pick))
 

time: 21.1 us -> 19.4 us (0.919)
  local copies, waits for them, and re-layouts: 1.67 us -> 0.71 us
  Pallas kernels: 19.3 us -> 18.6 us
    unnamed x1, local copies, waits for them, and re-layouts: 1.67 us -> 0.71 us
    pallas_call x1, Pallas kernels: 19.3 us -> 18.6 us  [quad_shards(): pl.pallas_call(functools.partial(kernel, groups, crates), out_shape=pltpu...]
where the time goes in v3:
time: 19.4 us; the launch traced here: 19.3 us
  Pallas kernels  18.6 us (96%)
  local copies, waits for them, and re-layouts  0.71 us (4%)
    pallas_call x1, Pallas kernels, quad_shards(): pl.pallas_call(functools.partial(kernel, groups, crates), out_shape=pltpu...  18.6 us
    unnamed x1, local copies, waits for them, and re-layouts  0.71 us

profile of v3, /device:TPU:0, one launch (start us, length us, event | category | flops | bytes accessed | tf_op | source)
XLA Modules:
  0.0 19.3 jit_solution(16896869977939659304)
XLA Ops:
  0.0 18.6 %shard_map.55 = f32[16,2,16,64]{3,2,1,0:T(8,128)S(1)} custom-call(bf16[8288,128]{1,0:T(8,128)(2,1)} %bitcast.6, bf16[2,256]{1,0:T(2,128)(2,1)} %bitcast.7, f32[4,32,128]{2,1,0:T(8,128)} %constant.6.clone.window_hbm, bf16[256,2048]{1,0:T(8,128)(2,1)} %constant.7.clone.table_hbm, bf16[512,256]{1,0:T(8,128)(2,1)} %constant.8.clone.pick_hbm), custom_call_target="tpu_custom_call" | custom-call | tf_op jit(solution)/shard_map/pallas_call | solution.py:258
  18.6 0.7 %copy.8 = f32[16,2,16,64]{3,2,1,0:T(8,128)} copy(f32[16,2,16,64]{3,2,1,0:T(8,128)S(1)} %shard_map.55) | data formatting | bytes 262144

commit v4 on v3

--- a/solution.py
+++ b/solution.py
@@ -106,17 +106,20 @@
         )
     ]
     head = pieces // CHUNKS
-    for item in [*sides[:3], *loads[:head], sides[3], *loads[head:]]:
+    for item in [*sides[:3], *loads[:head]]:
         item.start()
 
     barrier = pltpu.get_barrier_semaphore()
 
-    @pl.loop(1, n)
-    def _(k):
-        other = lax.rem(own + k, n)
+    near_g = [lax.rem(g + k, groups) for k in range(groups)]
+    near_r = [lax.rem(r + k, crates) for k in range(crates)]
+    for k in reversed(range(1, n)):
         pl.semaphore_signal(
-            barrier, inc=1, device_id=(other // crates, lax.rem(other, crates)), device_id_type=MESH
+            barrier, inc=1, device_id=(near_g[k // crates], near_r[k % crates]), device_id_type=MESH
         )
+
+    for item in [sides[3], *loads[head:]]:
+        item.start()
 
     sides[1].wait()
     sides[2].wait()
@@ -200,30 +203,35 @@
 
         arrived[h, source] = outgoing[h, own]
 
+    inputs = 2 * n
+    rows = inputs // crates
+    sums = [0.0] * QUAD
     for h in range(CHUNKS):
         pltpu.make_async_copy(outgoing.at[h, rest], arrived.at[h, rest], recv_sem.at[h]).wait()
         wide[h, : n * 4 * QUAD] = arrived[h].astype(jnp.float32).reshape(n * 4 * QUAD, LANES)
-
-    inputs = 2 * n
-    rows = inputs // crates
+        for q in range(QUAD):
+            real = wide[h, pl.ds(q, inputs, stride=2 * QUAD), :]
+            imag = wide[h, pl.ds(QUAD + q, inputs, stride=2 * QUAD), :]
+            left = jnp.concatenate([real, imag], axis=1).astype(jnp.bfloat16)
+            turned = jnp.concatenate([-imag, real], axis=1).astype(jnp.bfloat16)
+            right = jnp.concatenate([left, turned], axis=0)
+            sums[q] = sums[q] + lax.dot_general(
+                left, right, NT, preferred_element_type=jnp.float32
+            )
     for q in range(QUAD):
-        real = [wide[h, pl.ds(q, inputs, stride=2 * QUAD), :] for h in range(CHUNKS)]
-        imag = [wide[h, pl.ds(QUAD + q, inputs, stride=2 * QUAD), :] for h in range(CHUNKS)]
-        left = jnp.concatenate(real + imag, axis=1).astype(jnp.bfloat16)
-        turned = jnp.concatenate([-x for x in imag] + real, axis=1).astype(jnp.bfloat16)
-        right = jnp.concatenate([left, turned], axis=0)
-        vis = lax.dot_general(left, right, NT, preferred_element_type=jnp.float32) * (1.0 / SPEC)
+        vis = sums[q] * (1.0 / SPEC)
         vis_out[:, q] = vis.reshape(crates, rows, 2 * inputs)
-        for k in range(1, crates):
-            other = lax.rem(r + k, crates)
-            pltpu.make_async_remote_copy(
-                src_ref=vis_out.at[other, q],
-                dst_ref=vis_in.at[r, q],
-                send_sem=vsend_sem,
-                recv_sem=vrecv_sem,
-                device_id=(g, other),
-                device_id_type=MESH,
-            ).start()
+
+    for k in range(1, crates):
+        other = lax.rem(r + k, crates)
+        pltpu.make_async_remote_copy(
+            src_ref=vis_out.at[other],
+            dst_ref=vis_in.at[r],
+            send_sem=vsend_sem,
+            recv_sem=vrecv_sem,
+            device_id=(g, other),
+            device_id_type=MESH,
+        ).start()
 
     vis_in[r] = vis_out[r]
     rest_v = pl.ds(0, crates - 1)
@@ -254,7 +262,7 @@
     stacked = volts.reshape(2, frames, LANES).transpose(1, 0, 2).reshape(2 * frames, LANES)
     hbm = pl.BlockSpec(memory_space=pltpu.HBM)
     vmem = pl.BlockSpec(memory_space=pltpu.VMEM)
-    pieces = 4
+    pieces = 2
     return pl.pallas_call(
         functools.partial(kernel, groups, crates),
         out_shape=pltpu.VMEM((crates * QUAD, 2, rows, inputs), jnp.float32),

time: 19.4 us -> 19.1 us (0.985)
  Pallas kernels: 18.6 us -> 18.2 us
    pallas_call x1, Pallas kernels: 18.6 us -> 18.2 us  [quad_shards(): pl.pallas_call(functools.partial(kernel, groups, crates), out_shape=pltpu...]
where the time goes in v4:
time: 19.1 us; the launch traced here: 18.9 us
  Pallas kernels  18.2 us (95%)
  local copies, waits for them, and re-layouts  0.71 us (4%)
    pallas_call x1, Pallas kernels, quad_shards(): pl.pallas_call(functools.partial(kernel, groups, crates), out_shape=pltpu...  18.2 us
    unnamed x1, local copies, waits for them, and re-layouts  0.71 us

profile of v4, /device:TPU:0, one launch (start us, length us, event | category | flops | bytes accessed | tf_op | source)
XLA Modules:
  0.0 18.9 jit_solution(11027655517747839761)
XLA Ops:
  0.0 18.2 %shard_map.55 = f32[16,2,16,64]{3,2,1,0:T(8,128)S(1)} custom-call(bf16[8288,128]{1,0:T(8,128)(2,1)} %bitcast.6, bf16[2,256]{1,0:T(2,128)(2,1)} %bitcast.7, f32[4,32,128]{2,1,0:T(8,128)} %constant.6.clone.window_hbm, bf16[256,2048]{1,0:T(8,128)(2,1)} %constant.7.clone.table_hbm, bf16[512,256]{1,0:T(8,128)(2,1)} %constant.8.clone.pick_hbm), custom_call_target="tpu_custom_call" | custom-call | tf_op jit(solution)/shard_map/pallas_call | solution.py:266
  18.2 0.7 %copy.8 = f32[16,2,16,64]{3,2,1,0:T(8,128)} copy(f32[16,2,16,64]{3,2,1,0:T(8,128)S(1)} %shard_map.55) | data formatting | bytes 262144
